TPU v7x, 256 devices: a whole 4x4x8 slice. The times are simulated.
256 devices in a mesh: group: 32 (over x, y, core), tensor: 8 (over z).
Axes of the slice: x: 4, y: 4, z: 8, core: 2. Of those that a mesh axis runs over, the one named last changes fastest.
Arguments:
- tokens: bfloat16 [65536, 8192], P('group', 'tensor'), may hold values from -6 to 6
- kv_weight: bfloat16 [8192, 2048], P('tensor'), may hold values from -0.0625 to 0.0625
- a_pool: bfloat16 [64, 8192, 128], P('group', 'tensor'), may hold values from -0.0625 to 0.0625
- b_pool: bfloat16 [64, 64, 2048], P('group', None, 'tensor'), may hold values from -0.75 to 0.75
- request_entry: int32 [448], P('group'), may hold values from 0 to 14, as said below
- block_request: int32 [32, 16], P('group'), may hold values from 0 to 13, never falling along the last dimension, each value on 1 to 2 neighbouring positions
- fetch_source: int32 [416, 1], P('group'), may hold values from 0 to 31; in each aligned block of 13 rows (0 to 12, 13 to 25, ...) no two rows name the same one
- fetch_slot: int32 [416], P('group'), may hold values from 0 to 1
Outputs:
- keys_values: bfloat16 [2048, 65536], P('tensor', 'group')
Inputs may be any that keep to these rules, and one draw needn't show every extreme that they name: Request r of group g uses entry request_entry[g * 14 + r] of the group's working table: entries below 2 are the group's own pool slots, entry 2 + f is the adapter of the group's f-th fetch; every fetch of a group is used by some request of it. `block_request`: requests cover whole blocks in order, each 1 to 2 blocks, some request exactly that many. The f-th fetch of group g reads slot fetch_slot[g * 13 + f] of the pool of group fetch_source[g * 13 + f, 0], which may be g itself; no group has more than 1 fetches from one source group, and some group has exactly 1.
All inputs are finite; a program needn't handle non-finite values.
Results may differ from a plain program's by a relative error of at most 0.02.
Values may be sent and summed in bfloat16 or wider, within the bound.
No kernel may reach another device: no remote copies, remote signals or barrier semaphores. Data moves between devices by JAX's collectives and lax.ppermute only.
A program may use at most 128 MiB of HBM per device.

v0:
```python
import jax
import jax.numpy as jnp
from jax import lax
from jax.sharding import PartitionSpec as P

HEAD = 128
CAP = 1


def per_device(
    tokens, kv_weight, a_pool, b_pool, request_entry, block_request, fetch_source, fetch_slot
):
    groups = lax.axis_size("group")
    token_rows = tokens.shape[0]
    blocks = block_request.shape[1]
    tile_lines = token_rows // blocks
    rank_width = b_pool.shape[1]
    local_column_span = b_pool.shape[2]
    source = fetch_source[:, 0]
    same_source = source[:, None] == source[None, :]
    position = jnp.sum(jnp.tril(same_source, -1).astype(jnp.int32), axis=1)
    peer_ids = jnp.arange(groups, dtype=jnp.int32)[:, None, None]
    lane_ids = jnp.arange(CAP, dtype=jnp.int32)[None, :, None]
    matches = (source[None, None, :] == peer_ids) & (position[None, None, :] == lane_ids)
    wanted = jnp.sum(jnp.where(matches, fetch_slot[None, None, :], 0), axis=2)
    requested = lax.all_to_all(wanted, "group", split_axis=0, concat_axis=0, tiled=True)
    outgoing_a = a_pool[requested]
    outgoing_b = b_pool[requested]
    arrived_a, arrived_b = (
        lax.all_to_all(outgoing_a, "group", split_axis=0, concat_axis=0, tiled=True),
        lax.all_to_all(outgoing_b, "group", split_axis=0, concat_axis=0, tiled=True),
    )
    fetched_a = arrived_a[source, position]
    fetched_b = arrived_b[source, position]
    working_a = jnp.concatenate([a_pool, fetched_a], axis=0)
    working_b = jnp.concatenate([b_pool, fetched_b], axis=0)
    block_entry = request_entry[block_request[0]]
    a_blocks = working_a[block_entry]
    x_blocks = tokens.reshape(blocks, tile_lines, tokens.shape[1])
    partial_value = jnp.einsum(
        "btd,bdr->btr", x_blocks, a_blocks, preferred_element_type=jnp.float32
    )
    shrink = lax.psum(partial_value.astype(jnp.bfloat16), "tensor")
    pretrained_output_total = lax.psum_scatter(
        lax.dot_general(
            kv_weight, tokens, (((0,), (1,)), ((), ())), preferred_element_type=jnp.float32
        ).astype(jnp.bfloat16),
        "tensor",
        scatter_dimension=0,
        tiled=True,
    ).astype(jnp.float32)
    lifting_factor_tiles = working_b[block_entry].reshape(
        blocks, rank_width, local_column_span // (2 * HEAD), 2, HEAD
    )
    bottleneck_partial_terms = shrink.reshape(blocks, tile_lines, 2, rank_width)
    adapter_correction = jnp.einsum(
        "kdfe,kerft->rftkd",
        bottleneck_partial_terms,
        lifting_factor_tiles,
        preferred_element_type=jnp.float32,
    )
    adapter_correction = adapter_correction.reshape(local_column_span, token_rows)
    return (pretrained_output_total + adapter_correction).astype(jnp.bfloat16)


def solution(mesh):
    placed = (
        P("group", "tensor"),
        P("tensor", None),
        P("group", "tensor", None),
        P("group", None, "tensor"),
        P("group"),
        P("group", None),
        P("group", None),
        P("group"),
    )
    return jax.shard_map(
        per_device, mesh=mesh, in_specs=placed, out_specs=P("tensor", "group"), check_vma=False
    )
```

profile of v0, /device:TPU:1, one launch (start us, length us, event | category | flops | bytes accessed | tf_op | source)
XLA Modules:
  0.0 361.9 jit_solution(12396944543742319591)
XLA Ops:
  6.5 0.0 copy-start
  6.5 0.9 convert_reduce_fusion
  7.5 0.8 fusion.5
  8.3 0.1 copy.27
  8.3 15.3 %all_to_all.19 = s32[32,1,1]{2,1,0:T(1,128)S(1)} all-to-all(s32[32,1,1]{2,1,0:T(1,128)S(1)} %copy.27), channel_id=1, replica_groups=mesh['group'=32,'tensor'=8] {'group'}, dimensions={0} | all-to-all | bytes 256 | tf_op jit(solution)/shard_map/all_to_all | solution.py:26
  23.7 0.7 fusion.3
  24.3 5.9 %gather_fusion.4 = bf16[32,1024,128]{2,1,0:T(8,128)(2,1)} fusion(bf16[2,1024,128]{2,1,0:T(8,128)(2,1)} %param.10, s32[1024]{0:T(1024)S(1)} %pad_clamp_fusion.2), kind=kCustom, calls=%fused_computation.4 | custom fusion | bytes 16777344 | tf_op jit(solution)/shard_map/gather | solution.py:27
  30.2 0.0 copy-start.4
  30.2 0.0 copy-start.3
  30.2 5.3 %all-to-all-start.2 = ((bf16[32,1,1024,128]{3,2,1,0:T(8,128)(2,1)}), bf16[32,1,1024,128]{3,2,1,0:T(8,128)(2,1)}, u32[]{:S(2)}, u32[]{:S(2)}) async-start(bf16[32,1,1024,128]{3,2,1,0:T(8,128)(2,1)} %bitcast.44), calls=%async_computation.3 | async-start | bytes 16777216 | tf_op jit(solution)/shard_map/all_to_all | solution.py:30
  35.6 0.0 copy-start.1
  35.6 0.0 all-reduce.2.cloned.1.call-start
  35.6 0.0 copy-done.4
  35.7 0.0 copy-done
  35.7 0.7 gather_fusion.2
  36.4 0.0 copy-done.3
  36.4 106.0 %all-to-all-done.2 = bf16[32,1,1024,128]{3,2,1,0:T(8,128)(2,1)} async-done(((bf16[32,1,1024,128]{3,2,1,0:T(8,128)(2,1)}), bf16[32,1,1024,128]{3,2,1,0:T(8,128)(2,1)}, u32[]{:S(2)}, u32[]{:S(2)}) %all-to-all-start.2) | async-done | bytes 8388640 | tf_op jit(solution)/shard_map/all_to_all | solution.py:30
  142.4 6.3 %gather_fusion.5 = bf16[13,1024,128]{2,1,0:T(8,128)(2,1)} fusion(bf16[32,1,1024,128]{3,2,1,0:T(8,128)(2,1)} %all-to-all-done.2, s32[13]{0:T(128)S(1)} %fusion.13), kind=kCustom, calls=%fused_computation.5 | custom fusion | bytes 6815848 | tf_op jit(solution)/shard_map/gather | solution.py:33
  148.6 0.0 copy-done.1
  148.6 4.2 %pad_maximum_fusion = bf16[15,1024,128]{2,1,0:T(8,128)(2,1)} fusion(bf16[13,1024,128]{2,1,0:T(8,128)(2,1)} %gather_fusion.5, bf16[2,1024,128]{2,1,0:T(8,128)(2,1)S(1)} %copy-done.1), kind=kLoop, calls=%fused_computation.8 | loop fusion | flops 1966080 | bytes 7864320 | tf_op jit(solution)/shard_map/concatenate | solution.py:35
  152.8 5.1 %gather_fusion.6 = bf16[16,1024,128]{2,1,0:T(8,128)(2,1)} fusion(bf16[15,1024,128]{2,1,0:T(8,128)(2,1)} %pad_maximum_fusion, s32[1024]{0:T(1024)S(1)} %pad_clamp_fusion), kind=kCustom, calls=%fused_computation.6 | custom fusion | bytes 8388672 | tf_op jit(solution)/shard_map/gather | solution.py:38
  157.9 4.9 %convolution_convert_fusion.1 = bf16[16,128,128]{2,1,0:T(8,128)(2,1)S(1)} fusion(bf16[16,1024,128]{2,1,0:T(8,128)(2,1)} %gather_fusion.6, bf16[16,128,1024]{2,1,0:T(8,128)(2,1)} %bitcast.47), kind=kOutput, calls=%fused_computation.12 | convolution fusion | flops 537133056 | bytes 8912896 | tf_op jit(solution)/shard_map/btd,bdr->btr/dot_general | solution.py:40
  162.9 0.8 copy.29
  163.7 0.0 all-reduce.2.cloned.1.call-update
  163.7 0.0 reduce-scatter.2.cloned.1.call-start
  163.8 14.1 %convolution_convert_fusion = bf16[2048,2048]{1,0:T(8,128)(2,1)} fusion(bf16[1024,2048]{1,0:T(8,128)(2,1)} %param.9, bf16[2048,1024]{1,0:T(8,128)(2,1)} %param.8), kind=kOutput, calls=%fused_computation.7 | convolution fusion | flops 8594128896 | bytes 16777216 | tf_op jit(solution)/shard_map/dot_general | solution.py:45
  177.9 0.0 copy-start.2
  177.9 0.0 reduce-scatter.2.cloned.1.call-update
  177.9 0.8 copy-done.2
  178.7 0.6 gather_fusion
  179.3 40.2 %all_to_all.20 = bf16[32,1,64,256]{3,2,1,0:T(8,128)(2,1)S(1)} all-to-all(bf16[32,1,64,256]{3,2,1,0:T(8,128)(2,1)S(1)} %bitcast.46), channel_id=1, replica_groups=mesh['group'=32,'tensor'=8] {'group'}, dimensions={0} | all-to-all | bytes 2097152 | tf_op jit(solution)/shard_map/all_to_all | solution.py:31
  219.5 0.6 gather_fusion.1
  220.2 0.6 gather_fusion.3
  220.8 30.6 %all-reduce.2.cloned.1.call-done = bf16[16,128,2,64]{1,3,0,2:T(8,128)(2,1)} async-done(((bf16[16,128,2,64]{1,3,0,2:T(8,128)(2,1)}), bf16[16,128,2,64]{1,3,0,2:T(8,128)(2,1)}) %all-reduce.2.cloned.1.call-update) | async-done | bytes 524304 | tf_op jit(solution)/shard_map/psum | solution.py:43
  251.4 1.5 convolution_bitcast_fusion
  252.9 1.2 copy.31
  254.2 97.9 %reduce-scatter.2.cloned.1.call-done = bf16[256,2048]{1,0:T(8,128)(2,1)} async-done(((bf16[2048,2048]{1,0:T(8,128)(2,1)}), bf16[256,2048]{1,0:T(8,128)(2,1)}) %reduce-scatter.2.cloned.1.call-update) | async-done | bytes 1048592 | tf_op jit(solution)/shard_map/reduce_scatter | solution.py:44
  352.1 3.0 fusion
  (9 shorter events, 0.1 us)
Async XLA Ops:
  6.5 29.1 %copy-start = (s32[14]{0:T(128)S(1)}, s32[14]{0:T(128)}, u32[]{:S(2)}) copy-start(s32[14]{0:T(128)} %param.12) | copy-start | bytes 172
  30.2 5.4 %copy-start.4 = (s32[1,16]{1,0:T(1,128)S(1)}, s32[1,16]{1,0:T(1,128)}, u32[]{:S(2)}) copy-start(s32[1,16]{1,0:T(1,128)} %param.13) | copy-start | bytes 196
  30.2 6.1 %copy-start.3 = (s32[13,1]{0,1:T(1,128)S(1)}, s32[13,1]{0,1:T(1,128)}, u32[]{:S(2)}) copy-start(s32[13,1]{0,1:T(1,128)} %param.14) | copy-start | bytes 160
  30.2 112.1 %all-to-all-start.2 = ((bf16[32,1,1024,128]{3,2,1,0:T(8,128)(2,1)}), bf16[32,1,1024,128]{3,2,1,0:T(8,128)(2,1)}, u32[]{:S(2)}, u32[]{:S(2)}) async-start(bf16[32,1,1024,128]{3,2,1,0:T(8,128)(2,1)} %bitcast.44), calls=%async_computation.3 | async-start | bytes 16777216 | tf_op jit(solution)/shard_map/all_to_all | solution.py:30
  35.6 113.1 %copy-start.1 = (bf16[2,1024,128]{2,1,0:T(8,128)(2,1)S(1)}, bf16[2,1024,128]{2,1,0:T(8,128)(2,1)}, u32[]{:S(2)}) copy-start(bf16[2,1024,128]{2,1,0:T(8,128)(2,1)} %param.10) | copy-start | bytes 1572868
  35.6 215.8 %all-reduce.2.cloned.1.call-start = ((), (), s32[]{:S(2)}) async-start(), calls=%async_computation.5 | async-start | bytes 1048576 | tf_op jit(solution)/shard_map/psum | solution.py:43
  163.7 188.3 %reduce-scatter.2.cloned.1.call-start = ((), (), s32[]{:S(2)}) async-start(), calls=%async_computation.4 | async-start | bytes 9437184 | tf_op jit(solution)/shard_map/reduce_scatter | solution.py:44
  177.9 0.8 copy-start.2
Sparse Core Ops, SparseCore 0:
  163.8 87.5 all-reduce.1
  254.1 97.9 reduce-scatter.1
where the time goes:
time: 362 us
  waiting for transfers between devices  235 us (65%)
  blocking collectives  55.5 us (15%)
  local copies, waits for them, and re-layouts  22.7 us (6%)
  matrix products  20.6 us (6%)
  between operations  13.5 us (4%)
  other arithmetic  9.65 us (3%)
  starting transfers between devices  5.43 us (2%)
    all_to_all x1, waiting for transfers between devices, per_device(): lax.all_to_all(outgoing_a, 'group', split_axis=0, concat_axis=0, tiled=True)  106 us
    reduce_scatter x1, waiting for transfers between devices, per_device(): lax.psum_scatter(lax.dot_general(kv_weight, tokens, (((0,), (1,)), ((), (...  97.9 us
    all_to_all x1, blocking collectives, per_device(): lax.all_to_all(outgoing_b, 'group', split_axis=0, concat_axis=0, tiled=True)  40.2 us
    psum x1, waiting for transfers between devices, per_device(): shrink = lax.psum(partial_value.astype(jnp.bfloat16), 'tensor')  30.6 us
    all_to_all x1, blocking collectives, per_device(): lax.all_to_all(wanted, 'group', split_axis=0, concat_axis=0, tiled=True)  15.3 us
    dot_general x1, matrix products, per_device(): lax.dot_general(kv_weight, tokens, (((0,), (1,)), ((), ())), preferred_el...  14.1 us
  transfers between devices with their start and end apart: 3, of which 3 were waited for; matrix products, arithmetic and copies ran while one was open for 5% of the time, Pallas kernels for 0%

commit v1 on v0

--- a/solution.py
+++ b/solution.py
@@ -40,7 +40,7 @@
     partial_value = jnp.einsum(
         "btd,bdr->btr", x_blocks, a_blocks, preferred_element_type=jnp.float32
     )
-    shrink = lax.psum(partial_value.astype(jnp.bfloat16), "tensor")
+    shrink = jnp.sum(lax.all_gather(partial_value.astype(jnp.bfloat16), "tensor"), axis=0)
     pretrained_output_total = lax.psum_scatter(
         lax.dot_general(
             kv_weight, tokens, (((0,), (1,)), ((), ())), preferred_element_type=jnp.float32

time: 362 us -> 344 us (0.950)
  waiting for transfers between devices: 235 us -> 214 us
    psum x1 -> x0, waiting for transfers between devices: 30.6 us -> none  [per_device(): shrink = lax.psum(partial_value.astype(jnp.bfloat16), 'tensor')]
    all_gather x0 -> x1, waiting for transfers between devices: none -> 16.6 us  [per_device(): lax.all_gather(partial_value.astype(jnp.bfloat16), 'tensor')]
    reduce_scatter x1, waiting for transfers between devices: 97.9 us -> 91.1 us  [per_device(): lax.psum_scatter(lax.dot_general(kv_weight, tokens, (((0,), (1,)), ((), (...]
  transfers between devices with their start and end apart: 3 -> 3, of which waited for: 3 -> 3; matrix products, arithmetic and copies ran while one was open for 5% -> 6% of each run, Pallas kernels for 0% -> 0%
where the time goes in v1:
time: 344 us
  waiting for transfers between devices  214 us (62%)
  blocking collectives  55.5 us (16%)
  local copies, waits for them, and re-layouts  23.2 us (7%)
  matrix products  19.5 us (6%)
  between operations  13.6 us (4%)
  other arithmetic  12.6 us (4%)
  starting transfers between devices  5.43 us (2%)
    all_to_all x1, waiting for transfers between devices, per_device(): lax.all_to_all(outgoing_a, 'group', split_axis=0, concat_axis=0, tiled=True)  106 us
    reduce_scatter x1, waiting for transfers between devices, per_device(): lax.psum_scatter(lax.dot_general(kv_weight, tokens, (((0,), (1,)), ((), (...  91.1 us
    all_to_all x1, blocking collectives, per_device(): lax.all_to_all(outgoing_b, 'group', split_axis=0, concat_axis=0, tiled=True)  40.2 us
    all_gather x1, waiting for transfers between devices, per_device(): lax.all_gather(partial_value.astype(jnp.bfloat16), 'tensor')  16.6 us
    all_to_all x1, blocking collectives, per_device(): lax.all_to_all(wanted, 'group', split_axis=0, concat_axis=0, tiled=True)  15.3 us
    dot_general x1, matrix products, per_device(): lax.dot_general(kv_weight, tokens, (((0,), (1,)), ((), ())), preferred_el...  14.1 us
  transfers between devices with their start and end apart: 3, of which 3 were waited for; matrix products, arithmetic and copies ran while one was open for 6% of the time, Pallas kernels for 0%

profile of v1, /device:TPU:1, one launch (start us, length us, event | category | flops | bytes accessed | tf_op | source)
XLA Modules:
  0.0 343.6 jit_solution(12225153038952985191)
XLA Ops:
  6.5 0.0 copy-start
  6.5 0.9 convert_reduce_fusion
  7.5 0.8 fusion.7
  8.3 0.1 copy.35
  8.3 15.3 %all_to_all.19 = s32[32,1,1]{2,1,0:T(1,128)S(1)} all-to-all(s32[32,1,1]{2,1,0:T(1,128)S(1)} %copy.35), channel_id=1, replica_groups=mesh['group'=32,'tensor'=8] {'group'}, dimensions={0} | all-to-all | bytes 256 | tf_op jit(solution)/shard_map/all_to_all | solution.py:26
  23.7 0.7 fusion.5
  24.3 5.9 %gather_fusion.4 = bf16[32,1024,128]{2,1,0:T(8,128)(2,1)} fusion(bf16[2,1024,128]{2,1,0:T(8,128)(2,1)} %param.10, s32[1024]{0:T(1024)S(1)} %pad_clamp_fusion.2), kind=kCustom, calls=%fused_computation.4 | custom fusion | bytes 16777344 | tf_op jit(solution)/shard_map/gather | solution.py:27
  30.2 0.0 copy-start.4
  30.2 0.0 copy-start.3
  30.2 5.3 %all-to-all-start.2 = ((bf16[32,1,1024,128]{3,2,1,0:T(8,128)(2,1)}), bf16[32,1,1024,128]{3,2,1,0:T(8,128)(2,1)}, u32[]{:S(2)}, u32[]{:S(2)}) async-start(bf16[32,1,1024,128]{3,2,1,0:T(8,128)(2,1)} %bitcast.44), calls=%async_computation.3 | async-start | bytes 16777216 | tf_op jit(solution)/shard_map/all_to_all | solution.py:30
  35.6 0.0 copy-start.1
  35.6 0.0 all-gather.3.cloned.1.call-start
  35.6 0.0 copy-done.4
  35.7 0.0 copy-done
  35.7 0.7 gather_fusion.2
  36.4 0.0 copy-done.3
  36.4 106.0 %all-to-all-done.2 = bf16[32,1,1024,128]{3,2,1,0:T(8,128)(2,1)} async-done(((bf16[32,1,1024,128]{3,2,1,0:T(8,128)(2,1)}), bf16[32,1,1024,128]{3,2,1,0:T(8,128)(2,1)}, u32[]{:S(2)}, u32[]{:S(2)}) %all-to-all-start.2) | async-done | bytes 8388640 | tf_op jit(solution)/shard_map/all_to_all | solution.py:30
  142.4 6.3 %gather_fusion.5 = bf16[13,1024,128]{2,1,0:T(8,128)(2,1)} fusion(bf16[32,1,1024,128]{3,2,1,0:T(8,128)(2,1)} %all-to-all-done.2, s32[13]{0:T(128)S(1)} %fusion.15), kind=kCustom, calls=%fused_computation.5 | custom fusion | bytes 6815848 | tf_op jit(solution)/shard_map/gather | solution.py:33
  148.6 0.0 copy-done.1
  148.6 4.2 %pad_maximum_fusion = bf16[15,1024,128]{2,1,0:T(8,128)(2,1)} fusion(bf16[13,1024,128]{2,1,0:T(8,128)(2,1)} %gather_fusion.5, bf16[2,1024,128]{2,1,0:T(8,128)(2,1)S(1)} %copy-done.1), kind=kLoop, calls=%fused_computation.8 | loop fusion | flops 1966080 | bytes 7864320 | tf_op jit(solution)/shard_map/concatenate | solution.py:35
  152.8 5.1 %gather_fusion.6 = bf16[16,1024,128]{2,1,0:T(8,128)(2,1)} fusion(bf16[15,1024,128]{2,1,0:T(8,128)(2,1)} %pad_maximum_fusion, s32[1024]{0:T(1024)S(1)} %pad_clamp_fusion), kind=kCustom, calls=%fused_computation.6 | custom fusion | bytes 8388672 | tf_op jit(solution)/shard_map/gather | solution.py:38
  157.9 4.9 %fusion.1 = bf16[16,128,128]{1,2,0:T(8,128)(2,1)S(1)} fusion(bf16[16,1024,128]{2,1,0:T(8,128)(2,1)} %gather_fusion.6, bf16[16,128,1024]{2,1,0:T(8,128)(2,1)} %bitcast.48), kind=kOutput, calls=%fused_computation.13 | convolution fusion | flops 537133056 | bytes 8912896 | tf_op jit(solution)/shard_map/btd,bdr->btr/dot_general | solution.py:40
  162.9 1.0 copy.37
  163.9 0.0 all-gather.3.cloned.1.call-update
  163.9 0.0 reduce-scatter.2.cloned.1.call-start
  164.0 14.1 %convolution_convert_fusion = bf16[2048,2048]{1,0:T(8,128)(2,1)} fusion(bf16[1024,2048]{1,0:T(8,128)(2,1)} %param.9, bf16[2048,1024]{1,0:T(8,128)(2,1)} %param.8), kind=kOutput, calls=%fused_computation.7 | convolution fusion | flops 8594128896 | bytes 16777216 | tf_op jit(solution)/shard_map/dot_general | solution.py:45
  178.1 0.0 copy-start.2
  178.1 0.0 reduce-scatter.2.cloned.1.call-update
  178.1 0.8 copy-done.2
  178.9 0.6 gather_fusion
  179.5 40.2 %all_to_all.20 = bf16[32,1,64,256]{3,2,1,0:T(8,128)(2,1)S(1)} all-to-all(bf16[32,1,64,256]{3,2,1,0:T(8,128)(2,1)S(1)} %bitcast.47), channel_id=1, replica_groups=mesh['group'=32,'tensor'=8] {'group'}, dimensions={0} | all-to-all | bytes 2097152 | tf_op jit(solution)/shard_map/all_to_all | solution.py:31
  219.7 0.6 gather_fusion.1
  220.4 0.6 gather_fusion.3
  221.0 16.6 %all-gather.3.cloned.1.call-done = bf16[128,128,128]{2,1,0:T(8,128)(2,1)} async-done(((bf16[16,128,128]{2,1,0:T(8,128)(2,1)}), bf16[128,128,128]{2,1,0:T(8,128)(2,1)}) %all-gather.3.cloned.1.call-update) | async-done | bytes 4194320 | tf_op jit(solution)/shard_map/all_gather | solution.py:43
  237.6 3.0 reduce_sum.35
  240.6 0.3 copy.38
  240.9 0.5 convolution_bitcast_fusion
  241.4 1.2 copy.41
  242.6 91.1 %reduce-scatter.2.cloned.1.call-done = bf16[256,2048]{1,0:T(8,128)(2,1)} async-done(((bf16[2048,2048]{1,0:T(8,128)(2,1)}), bf16[256,2048]{1,0:T(8,128)(2,1)}) %reduce-scatter.2.cloned.1.call-update) | async-done | bytes 1048592 | tf_op jit(solution)/shard_map/reduce_scatter | solution.py:44
  333.7 3.0 fusion
  (9 shorter events, 0.1 us)
Async XLA Ops:
  6.5 29.1 %copy-start = (s32[14]{0:T(128)S(1)}, s32[14]{0:T(128)}, u32[]{:S(2)}) copy-start(s32[14]{0:T(128)} %param.12) | copy-start | bytes 172
  30.2 5.4 %copy-start.4 = (s32[1,16]{1,0:T(1,128)S(1)}, s32[1,16]{1,0:T(1,128)}, u32[]{:S(2)}) copy-start(s32[1,16]{1,0:T(1,128)} %param.13) | copy-start | bytes 196
  30.2 6.1 %copy-start.3 = (s32[13,1]{0,1:T(1,128)S(1)}, s32[13,1]{0,1:T(1,128)}, u32[]{:S(2)}) copy-start(s32[13,1]{0,1:T(1,128)} %param.14) | copy-start | bytes 160
  30.2 112.1 %all-to-all-start.2 = ((bf16[32,1,1024,128]{3,2,1,0:T(8,128)(2,1)}), bf16[32,1,1024,128]{3,2,1,0:T(8,128)(2,1)}, u32[]{:S(2)}, u32[]{:S(2)}) async-start(bf16[32,1,1024,128]{3,2,1,0:T(8,128)(2,1)} %bitcast.44), calls=%async_computation.3 | async-start | bytes 16777216 | tf_op jit(solution)/shard_map/all_to_all | solution.py:30
  35.6 113.1 %copy-start.1 = (bf16[2,1024,128]{2,1,0:T(8,128)(2,1)S(1)}, bf16[2,1024,128]{2,1,0:T(8,128)(2,1)}, u32[]{:S(2)}) copy-start(bf16[2,1024,128]{2,1,0:T(8,128)(2,1)} %param.10) | copy-start | bytes 1572868
  35.6 202.0 %all-gather.3.cloned.1.call-start = ((), (), s32[]{:S(2)}) async-start(), calls=%async_computation.5 | async-start | bytes 4718592 | tf_op jit(solution)/shard_map/all_gather | solution.py:43
  163.9 169.8 %reduce-scatter.2.cloned.1.call-start = ((), (), s32[]{:S(2)}) async-start(), calls=%async_computation.4 | async-start | bytes 9437184 | tf_op jit(solution)/shard_map/reduce_scatter | solution.py:44
  178.1 0.8 copy-start.2
Sparse Core Ops, SparseCore 0:
  164.0 73.5 all-gather.2
  240.1 93.5 reduce-scatter.1
